TPU v7x, 256 devices: a whole 4x4x8 slice. The times are simulated.
256 devices in a mesh: prow: 16 (over x_hi, z), pcol: 16 (over y, x_lo, core).
Axes of the slice: x: 4 (x_hi: 2, x_lo: 2; x = x_hi * 2 + x_lo), y: 4, z: 8, core: 2. Of those that a mesh axis runs over, the one named last changes fastest.
Arguments:
- ancestor_inverse: float32 [10, 16, 128, 10, 16, 128], P(None, 'prow', None, None, 'pcol'), may hold values from -6 to 6
- factor_panel: float32 [2, 10, 16, 128, 256], P(None, None, 'prow'), may hold values from -0.046875 to 0.046875
- structure: int32 [2, 120], replicated, may hold values from 0 to 159, as said below
- block_map: int32 [160], replicated, may hold values from 0 to 159, each once
- diag_inverse: float32 [2, 256, 256], replicated, may hold values from -6 to 6
Outputs:
- ancestor_columns: float32 [2, 16, 16, 80, 256], P(None, 'prow', 'pcol')
- diag_block: float32 [2, 256, 256], replicated
Inputs may be any that keep to these rules, and one draw needn't show every extreme that they name: `structure`: each row lists 120 different ancestor blocks in increasing order; the first is block 0 and the last is block 159 in every row.
All inputs are finite; a program needn't handle non-finite values.
Results may differ from a plain program's by a relative error of at most 0.00007.
Values sent between devices are 32-bit elements; how exact they have to be, the bound alone decides.
A program may use at most 128 MiB of HBM per device.

v0:
```python
import jax
import jax.numpy as jnp
from jax import lax
from jax.sharding import PartitionSpec as P


def broadcast(value, axis, source):
    kept = jnp.where(lax.axis_index(axis) == source, value, 0).astype(value.dtype)
    return lax.psum(kept, axis)


def local(ancestor_inverse, factor_panel, structure, block_map, diag_inverse):
    row_count = lax.axis_size("prow")
    col_count = lax.axis_size("pcol")
    row_position = lax.axis_index("prow")
    col_place = lax.axis_index("pcol")
    row_blocks = ancestor_inverse.shape[0]
    block_rows = ancestor_inverse.shape[2]
    col_blocks = ancestor_inverse.shape[3]
    width = factor_panel.shape[-1]
    blocks = block_map.shape[0]
    local_rows = row_blocks * block_rows
    share_rows = local_rows // col_count
    matrix = ancestor_inverse.reshape(local_rows, col_blocks * block_rows)
    chosen = structure[:, :, None] == jnp.arange(blocks, dtype=jnp.int32)[None, None, :]
    structure_slots = jnp.sum(jnp.where(chosen, block_map[None, None, :], 0), axis=2)
    own_slots = jnp.arange(row_blocks, dtype=jnp.int32) * row_count + row_position
    live_mask = jnp.any(structure_slots[:, :, None] == own_slots[None, None, :], axis=1).astype(
        jnp.float32
    )
    masked = factor_panel[:, :, 0] * live_mask[:, :, None, None]
    row_live = jnp.repeat(live_mask, block_rows, axis=1)
    share_live = lax.dynamic_slice_in_dim(row_live, col_place * share_rows, share_rows, 1)

    def supernodes(panel_cluster, live_group, diag_group):
        members = panel_cluster.shape[0]
        own_panel = jnp.transpose(panel_cluster, (1, 2, 0, 3)).reshape(
            row_blocks, block_rows, members * width
        )
        pieces = [broadcast(own_panel, "prow", col_place + 0 * col_count)]
        column_panel = jnp.stack(pieces, axis=1).reshape(col_blocks * block_rows, members * width)
        summed = lax.psum_scatter(
            jnp.dot(
                matrix,
                column_panel,
                precision=lax.Precision.HIGHEST,
                preferred_element_type=jnp.float32,
            ),
            "pcol",
            scatter_dimension=0,
            tiled=True,
        )
        column_list = (
            -summed.reshape(share_rows, members, width) * jnp.transpose(live_group)[:, :, None]
        )
        owned_row_list = lax.dynamic_slice_in_dim(
            own_panel.reshape(local_rows, members, width), col_place * share_rows, share_rows, 0
        )
        nearby_terms = jnp.einsum(
            "thf,thx->hfx", owned_row_list, column_list, precision=lax.Precision.HIGHEST
        )
        diag_terms = lax.psum(nearby_terms, ("prow", "pcol"))
        return (jnp.transpose(column_list, (1, 0, 2)), diag_group - diag_terms)

    first_cols, first_diag = supernodes(masked[0:1], share_live[0:1], diag_inverse[0:1])
    second_cols, second_diag = supernodes(masked[1:2], share_live[1:2], diag_inverse[1:2])
    result_columns = jnp.concatenate([first_cols, second_cols], axis=0)
    diagonal = jnp.concatenate([first_diag, second_diag], axis=0)
    return (result_columns[:, None, None], diagonal)


def solution(mesh):
    in_specs = (
        P(None, "prow", None, None, "pcol", None),
        P(None, None, "prow", None, None),
        P(),
        P(),
        P(),
    )
    out_specs = (P(None, "prow", "pcol", None, None), P())
    return jax.shard_map(local, mesh=mesh, in_specs=in_specs, out_specs=out_specs, check_vma=False)
```

profile of v0, /device:TPU:1, one launch (start us, length us, event | category | flops | bytes accessed | tf_op | source)
XLA Modules:
  0.0 591.7 jit_solution(6482175534156847875)
XLA Ops:
  7.2 0.0 all-reduce.7.cloned.1.call-start
  7.2 0.8 select_reduce_fusion
  8.0 0.2 compare_reduce_fusion
  8.2 2.0 bitcast_multiply_fusion
  10.3 2.1 fusion.22
  12.4 0.0 all-reduce.7.cloned.1.call-update
  12.4 0.0 reduce-scatter.7.cloned.1.call-start
  12.5 70.9 %reduce = f32[10,128,10,128]{3,2,1,0:T(8,128)} reduce(f32[10,1,128,10,1,128]{5,4,3,2,1,0:T(1,128)} %param.5, f32[]{:T(128)} %constant.21), dimensions={1,4}, to_apply=%param.5.reduce_sub_computation | reduce | bytes 13107204 | tf_op args[0]
  83.4 88.7 %all-reduce.7.cloned.1.call-done = (f32[1280,256]{1,0:T(8,128)}, f32[1280,256]{1,0:T(8,128)}) async-done(((f32[1280,256]{1,0:T(8,128)}, f32[1280,256]{1,0:T(8,128)}), (f32[1280,256]{1,0:T(8,128)}, f32[1280,256]{1,0:T(8,128)})) %all-reduce.7.cloned.1.call-update) | async-done | bytes 2621456 | tf_op jit(solution)/shard_map/psum | solution.py:9
  172.1 15.9 %fusion.6 = f32[1280,256]{0,1:T(8,128)S(1)} fusion(f32[1280,256]{1,0:T(8,128)} %get-tuple-element.13, f32[160,8,10,128]{3,2,1,0:T(8,128)} %bitcast.50), kind=kOutput, calls=%fused_computation.6 | convolution fusion | flops 5033164800 | bytes 9175040 | tf_op jit(solution)/shard_map/dot_general | solution.py:43
  188.1 1.5 copy.11
  189.5 0.0 reduce-scatter.7.cloned.1.call-update
  189.6 0.3 reduce-scatter.9.cloned.1.call-start
  189.8 15.9 %fusion.9 = f32[1280,256]{0,1:T(8,128)S(1)} fusion(f32[1280,256]{1,0:T(8,128)} %get-tuple-element.12, f32[160,8,10,128]{3,2,1,0:T(8,128)} %bitcast.51), kind=kOutput, calls=%fused_computation.7 | convolution fusion | flops 5033164800 | bytes 9175040 | tf_op jit(solution)/shard_map/dot_general | solution.py:43
  205.8 1.5 copy.13
  207.2 0.0 reduce-scatter.9.cloned.1.call-update
  207.3 0.0 all-reduce.5.cloned.1.call-start
  207.3 0.1 broadcast_bitcast_fusion
  207.4 0.1 constant_dynamic-slice_fusion
  207.5 50.5 %reduce-scatter.7.cloned.1.call-done = f32[80,256]{1,0:T(8,128)} async-done(((f32[1280,256]{1,0:T(8,128)}), f32[80,256]{1,0:T(8,128)}) %reduce-scatter.7.cloned.1.call-update) | async-done | bytes 81936
  258.0 1.0 copy.12
  259.0 2.0 convolution_bitcast_fusion.1
  261.0 0.0 copy-start
  261.0 62.9 %reduce-scatter.9.cloned.1.call-done = f32[80,256]{1,0:T(8,128)} async-done(((f32[1280,256]{1,0:T(8,128)}), f32[80,256]{1,0:T(8,128)}) %reduce-scatter.9.cloned.1.call-update) | async-done | bytes 81936
  323.9 1.0 copy.14
  324.9 1.1 convolution_bitcast_fusion
  326.0 0.0 all-reduce.5.cloned.1.call-update
  326.1 0.8 copy.10
  326.9 256.3 %all-reduce.5.cloned.1.call-done = (f32[1,256,256]{2,1,0:T(8,128)}, f32[1,256,256]{2,1,0:T(8,128)}) async-done(((f32[1,256,256]{2,1,0:T(8,128)}, f32[1,256,256]{2,1,0:T(8,128)}), (f32[1,256,256]{2,1,0:T(8,128)}, f32[1,256,256]{2,1,0:T(8,128)})) %all-reduce.5.cloned.1.call-update) | async-done | bytes 524304 | tf_op jit(solution)/shard_map/psum | solution.py:62
  583.2 0.0 copy-done
  583.2 1.1 slice_subtract_fusion.1
  584.3 0.8 pad_maximum_fusion
  (7 shorter events, 0.1 us)
Async XLA Ops:
  7.2 165.0 %all-reduce.7.cloned.1.call-start = ((), (), s32[]{:S(2)}) async-start(), calls=%async_computation.5 | async-start | bytes 5242880 | tf_op jit(solution)/shard_map/psum | solution.py:9
  12.4 245.6 %reduce-scatter.7.cloned.1.call-start = ((), (), s32[]{:S(2)}) async-start(), calls=%async_computation.2 | async-start | bytes 1392640
  189.6 134.4 %reduce-scatter.9.cloned.1.call-start = ((), (), s32[]{:S(2)}) async-start(), calls=%async_computation.3 | async-start | bytes 1392640
  207.3 375.9 %all-reduce.5.cloned.1.call-start = ((), (), s32[]{:S(2)}) async-start(), calls=%async_computation.4 | async-start | bytes 1048576 | tf_op jit(solution)/shard_map/psum | solution.py:62
  261.0 322.2 %copy-start = (f32[2,256,256]{2,1,0:T(8,128)S(1)}, f32[2,256,256]{2,1,0:T(8,128)}, u32[]{:S(2)}) copy-start(f32[2,256,256]{2,1,0:T(8,128)} %param.9) | copy-start | bytes 1572868
Sparse Core Ops, SparseCore 0:
  12.6 159.5 all-reduce.6
  189.7 68.2 reduce-scatter.6
  260.5 63.3 reduce-scatter.8
  330.0 253.1 all-reduce.4
where the time goes:
time: 593 us; the launch traced here: 592 us
  waiting for transfers between devices  459 us (77%)
  other arithmetic  78.1 us (13%)
  matrix products  35 us (6%)
  between operations  13.9 us (2%)
    psum x1, waiting for transfers between devices, supernodes(): diag_terms = lax.psum(nearby_terms, ('prow', 'pcol'))  256 us
    unnamed x6, waiting for transfers between devices  113 us
    psum x1, waiting for transfers between devices, broadcast(): return lax.psum(kept, axis)  88.7 us
    unnamed x1, other arithmetic  70.9 us
    dot_general x2, matrix products, supernodes(): jnp.dot(matrix, column_panel, precision=lax.Precision.HIGHEST, preferred_...  31.9 us
  transfers between devices with their start and end apart: 4, of which 4 were waited for; matrix products, arithmetic and copies ran while one was open for 16% of the time, Pallas kernels for 0%

commit v1 on v0

v1 whole, which is shorter than its diff:
```python
import functools

import jax
import jax.numpy as jnp
from jax import lax
from jax.experimental import pallas as pl
from jax.experimental.pallas import tpu as pltpu
from jax.sharding import PartitionSpec as P

MESH = pl.DeviceIdType.MESH
F32 = jnp.float32
BF16 = jnp.bfloat16

RING = 8
SUBS = 2
ROWS = 64 // SUBS
STEPS = 2 * 10 * SUBS
LAG = 3
WAIT_A = 8
SHARED = True


def split(value):
    high = value.astype(BF16)
    return high, (value - high.astype(F32)).astype(BF16)


def three_dots(a_high, a_low, b_high, b_low):
    dot = functools.partial(jnp.dot, preferred_element_type=F32)
    return dot(a_high, b_high) + (dot(a_high, b_low) + dot(a_low, b_high))


def kernel(
    live_own, live_col, a_hbm, panel_hbm,
    y_out, d_out,
    a_raw, a_high, a_low, own, own_high, own_low, x, x_high, x_low,
    y, y_peer, y_send, y_recv, d_part, d_peer, d_send, d_recv, d_pair, d_ring,
    load_sem, z_ssem, z_rsem, x_ssem, x_rsem, c_ssem, c_rsem, y_ssem, y_rsem, d_ssem, d_rsem, p_ssem, p_rsem,
    r_ssem, r_rsem, g_ssem, g_rsem,
):
    p = lax.axis_index("prow")
    q = lax.axis_index("pcol")
    half = p // RING
    z = p % RING
    place = q // 2
    core = q % 2
    root_half = q // RING
    hops = (z - q % RING + RING) % RING
    on_root = half == root_half

    across = ((1 - half) * RING + z, q)
    sibling = (p, place * 2 + 1 - core)

    def ring(step):
        return (half * RING + (z + step) % RING, q)

    def chip(step):
        return (p, ((place + step) % 8) * 2 + core)

    load_own = pltpu.make_async_copy(panel_hbm, own, load_sem.at[0])
    load_own.start()
    load_root = pltpu.make_async_copy(panel_hbm, x, load_sem.at[1])

    @pl.when(p == q)
    def _():
        load_root.start()

    load_a = pltpu.make_async_copy(a_hbm, a_raw, load_sem.at[2])
    load_a.start()

    barrier = pltpu.get_barrier_semaphore()
    partners = [across, sibling] + [ring(i) for i in range(1, RING)] + [chip(i) for i in range(1, 8)]
    for partner in partners:
        pl.semaphore_signal(barrier, inc=1, device_id=partner, device_id_type=MESH)
    pl.semaphore_wait(barrier, len(partners))

    @pl.when(p == q)
    def _():
        load_root.wait()

    def chunk(way, s):
        block = s // SUBS
        row = way * 64 + (s % SUBS) * ROWS
        return x.at[block // 10, block % 10, pl.ds(row, ROWS)]

    def z_copy(way, s):
        return pltpu.make_async_remote_copy(
            src_ref=chunk(way, s), dst_ref=chunk(way, s), send_sem=z_ssem.at[way, s], recv_sem=z_rsem.at[way, s],
            device_id=ring(1 if way == 0 else RING - 1), device_id_type=MESH,
        )

    def x_copy(way, s):
        return pltpu.make_async_remote_copy(
            src_ref=chunk(way, s), dst_ref=chunk(way, s), send_sem=x_ssem.at[way, s], recv_sem=x_rsem.at[way, s],
            device_id=across, device_id_type=MESH,
        )

    def roles(way, s):
        if SHARED:
            kind = s % 3
            both = kind == 2
            carries = both | (on_root & (kind == 0)) | (jnp.logical_not(on_root) & (kind == 1))
        else:
            both = jnp.bool_(True)
            carries = jnp.bool_(True)
        done = hops if way == 0 else (RING - hops) % RING
        to_z = carries & (done < RING - 1)
        to_x = jnp.where(hops == 0, on_root, carries & jnp.logical_not(both))
        return carries, to_z, to_x

    def event(way, s):
        carries, to_z, to_x = roles(way, s)

        @pl.when((hops == 0) & jnp.logical_not(on_root))
        def _():
            x_copy(way, s).wait_recv()

        @pl.when((hops != 0) & carries)
        def _():
            z_copy(way, s).wait_recv()

        @pl.when(to_z)
        def _():
            z_copy(way, s).start()

        @pl.when(to_x)
        def _():
            x_copy(way, s).start()

    shift = jnp.where(hops == 0, 0, (RING - 2 * hops) * LAG)
    late_up = jnp.maximum(0, -shift)
    late_down = jnp.maximum(0, shift)

    def split_a(i):
        for col in range(10):
            high, low = split(a_raw[pl.ds(i * 320 + col, 32, stride=10), :])
            rows = pl.ds(pl.multiple_of(i * 32, 32), 32)
            a_high[rows, col * 128 : (col + 1) * 128] = high
            a_low[rows, col * 128 : (col + 1) * 128] = low

    def stream(t, carry):
        for way, late in ((0, late_up), (1, late_down)):
            s = t - late

            @pl.when((s >= 0) & (s < STEPS))
            def _():
                event(way, s)

        @pl.when(t == WAIT_A)
        def _():
            load_a.wait()

        @pl.when((t >= WAIT_A) & (t < WAIT_A + 40))
        def _():
            split_a(t - WAIT_A)

        return carry

    lax.fori_loop(0, max(STEPS + 6 * LAG, WAIT_A + 40), stream, 0)

    load_own.wait()

    def arrived(s, carry):
        for way in range(2):
            carries, _, _ = roles(way, s)

            @pl.when((hops != 0) & jnp.logical_not(carries))
            def _():
                x_copy(way, s).wait_recv()

        return carry

    if SHARED:
        lax.fori_loop(0, STEPS, arrived, 0)

    for k in range(2):

        def to_bf16(r, carry):
            rows = pl.ds(pl.multiple_of(r * 128, 128), 128)
            high, low = split(x[k, r] * live_col[k, r])
            x_high[rows] = high
            x_low[rows] = low
            high, low = split((own[k, r] * live_own[k, r]).T)
            own_high[:, rows] = high
            own_low[:, rows] = low
            return carry

        lax.fori_loop(0, 10, to_bf16, 0)

        def rows_of_y(m, carry):
            rows = pl.ds(pl.multiple_of(m * 160, 32), 160)
            part = three_dots(a_high[rows], a_low[rows], x_high[...], x_low[...])
            y[k, m] = part.reshape(2, 80, 256)
            return carry

        lax.fori_loop(0, 8, rows_of_y, 0)
        y_high, y_low = split(y[k].reshape(1280, 256))
        d_part[k] = three_dots(own_high[...], own_low[...], y_high, y_low).reshape(8, 32, 256)

    def remote(src, dst, send, recv, device):
        return pltpu.make_async_remote_copy(
            src_ref=src, dst_ref=dst, send_sem=send, recv_sem=recv, device_id=device, device_id_type=MESH
        )

    peer_d = remote(d_part.at[1 - core], d_peer, c_ssem.at[0], c_rsem.at[0], sibling)
    peer_y = remote(y.at[:, :, 1 - core], y_peer, c_ssem.at[1], c_rsem.at[1], sibling)
    peer_d.start()
    peer_y.start()
    peer_d.wait()
    for i in range(8):
        d_send[i] = d_part[core, i] + d_peer[i]
    d_copies = []
    for step in range(1, 8):
        to = (place + step) % 8
        copy = remote(d_send.at[to], d_recv.at[place], d_ssem.at[step], d_rsem.at[step], chip(step))
        copy.start()
        d_copies.append(copy)
    peer_y.wait()
    for i in range(8):
        for k in range(2):
            y_send[i, k] = y[k, i, core] + y_peer[k, i]
    y_copies = []
    for step in range(1, 8):
        to = (place + step) % 8
        copy = remote(y_send.at[to], y_recv.at[place], y_ssem.at[step], y_rsem.at[step], chip(step))
        copy.start()
        y_copies.append(copy)

    d_recv[place] = d_send[place]
    for copy in d_copies:
        copy.wait()
    total = d_recv[0]
    for i in range(1, 8):
        total = total + d_recv[i]
    d_pair[0] = total
    pair = remote(d_pair.at[0], d_pair.at[1], p_ssem, p_rsem, across)
    pair.start()
    pair.wait()
    d_ring[z] = d_pair[0] + d_pair[1]
    r_copies = []
    for step in range(1, RING):
        copy = remote(d_ring.at[z], d_ring.at[z], r_ssem.at[step], r_rsem.at[step], ring(step))
        copy.start()
        r_copies.append(copy)

    y_recv[place] = y_send[place]
    for copy in y_copies:
        copy.wait()
    for k in range(2):
        total = y_recv[0, k]
        for i in range(1, 8):
            total = total + y_recv[i, k]
        y_out[k] = total

    for copy in r_copies:
        copy.wait()
    total = d_ring[0]
    for i in range(1, RING):
        total = total + d_ring[i]
    d_out[core, place] = total
    g_copies = []
    for step in range(1, 8):
        copy = remote(d_out.at[core, place], d_out.at[core, place], g_ssem.at[step], g_rsem.at[step], chip(step))
        copy.start()
        g_copies.append(copy)
    for copy in g_copies:
        copy.wait()
    last = remote(d_out.at[core], d_out.at[core], c_ssem.at[2], c_rsem.at[2], sibling)
    last.start()
    last.wait()

    def sent(s, carry):
        for way in range(2):
            _, to_z, to_x = roles(way, s)

            @pl.when(to_z)
            def _():
                z_copy(way, s).wait_send()

            @pl.when(to_x)
            def _():
                x_copy(way, s).wait_send()

        return carry

    lax.fori_loop(0, STEPS, sent, 0)


def local(ancestor_inverse, factor_panel, structure, block_map, diag_inverse):
    row_count = lax.axis_size("prow")
    p = lax.axis_index("prow")
    q = lax.axis_index("pcol")
    blocks = block_map.shape[0]
    ids = jnp.arange(blocks, dtype=jnp.int32)
    in_structure = jnp.any(structure[:, :, None] == ids[None, None, :], axis=1)
    live = jnp.any(in_structure[:, :, None] & (block_map[None, :, None] == ids[None, None, :]), axis=1)
    live = live.astype(F32).reshape(2, 10, row_count)
    live_own = lax.dynamic_index_in_dim(live, p, 2, keepdims=False)
    live_col = lax.dynamic_index_in_dim(live, q, 2, keepdims=False)
    share_live = lax.dynamic_slice_in_dim(jnp.repeat(live_own, 128, axis=1), q * 80, 80, 1)

    dma = pltpu.SemaphoreType.DMA
    vmem = pltpu.VMEM
    columns, terms = pl.pallas_call(
        kernel,
        name="panel_product",
        out_shape=(jax.ShapeDtypeStruct((2, 80, 256), F32), jax.ShapeDtypeStruct((2, 8, 32, 256), F32)),
        in_specs=[pl.BlockSpec(memory_space=pltpu.SMEM)] * 2 + [pl.BlockSpec(memory_space=pl.ANY)] * 2,
        out_specs=(pl.BlockSpec(memory_space=pltpu.VMEM),) * 2,
        scratch_shapes=[
            vmem((12800, 128), F32), vmem((1280, 1280), BF16), vmem((1280, 1280), BF16),
            vmem((2, 10, 128, 256), F32), vmem((256, 1280), BF16), vmem((256, 1280), BF16),
            vmem((2, 10, 128, 256), F32), vmem((1280, 256), BF16), vmem((1280, 256), BF16),
            vmem((2, 8, 2, 80, 256), F32), vmem((2, 8, 80, 256), F32), vmem((8, 2, 80, 256), F32),
            vmem((8, 2, 80, 256), F32),
            vmem((2, 8, 32, 256), F32), vmem((8, 32, 256), F32), vmem((8, 32, 256), F32), vmem((8, 32, 256), F32),
            vmem((2, 32, 256), F32), vmem((RING, 32, 256), F32),
            dma((3,)), dma((2, STEPS)), dma((2, STEPS)), dma((2, STEPS)), dma((2, STEPS)), dma((3,)), dma((3,)),
            dma((8,)), dma((8,)), dma((8,)), dma((8,)), dma, dma, dma((RING,)), dma((RING,)), dma((8,)), dma((8,)),
        ],
        compiler_params=pltpu.CompilerParams(collective_id=0, has_side_effects=True, vmem_limit_bytes=50 * 2**20),
    )(live_own, live_col, ancestor_inverse.reshape(12800, 128), factor_panel.reshape(2, 10, 128, 256))
    columns = -columns * share_live[:, :, None]
    return columns[:, None, None], diag_inverse + terms.reshape(2, 256, 256)


def solution(mesh):
    in_specs = (
        P(None, "prow", None, None, "pcol", None),
        P(None, None, "prow", None, None),
        P(),
        P(),
        P(),
    )
    out_specs = (P(None, "prow", "pcol", None, None), P())
    return jax.shard_map(local, mesh=mesh, in_specs=in_specs, out_specs=out_specs, check_vma=False)
```

time: 593 us -> 136 us (0.23)
  waiting for transfers between devices: 459 us -> 0 us
  Pallas kernels: 0 us -> 130 us
  other arithmetic: 78.1 us -> 3.35 us
  matrix products: 35 us -> 0 us
  between operations: 13.9 us -> 0.67 us
    psum x2 -> x0, waiting for transfers between devices: 345 us -> none  [the longest x1 256 us: supernodes(): diag_terms = lax.psum(nearby_terms, ('prow', 'pcol'))]
    pallas_call x0 -> x1, Pallas kernels: none -> 130 us  [local(): pl.pallas_call(kernel, name='panel_product', out_shape=(jax.ShapeDtypeStr...]
    unnamed x6 -> x0, waiting for transfers between devices: 113 us -> none
    unnamed x1, other arithmetic: 70.9 us -> 0.76 us
    dot_general x4 -> x0, matrix products: 35 us -> none  [the longest x2 31.9 us: supernodes(): jnp.dot(matrix, column_panel, precision=lax.Precision.HIGHEST, preferred_...]
  transfers between devices with their start and end apart: 4 -> 0, of which waited for: 4 -> 0; matrix products, arithmetic and copies ran while one was open for 16% -> 0% of each run, Pallas kernels for 0% -> 0%
where the time goes in v1:
time: 136 us
  Pallas kernels  130 us (96%)
  other arithmetic  3.35 us (2%)
  local copies, waits for them, and re-layouts  2.16 us (2%)
    pallas_call x1, Pallas kernels, local(): pl.pallas_call(kernel, name='panel_product', out_shape=(jax.ShapeDtypeStr...  130 us

profile of v1, /device:TPU:1, one launch (start us, length us, event | category | flops | bytes accessed | tf_op | source)
XLA Modules:
  0.0 135.9 jit_solution(17531939038501079144)
XLA Ops:
  0.6 0.8 fusion
  1.5 0.8 iota_compare_fusion
  2.2 0.1 and_reduce_fusion
  2.4 0.1 reshape.45
  2.5 0.2 dynamic-slice_reduce_fusion
  2.6 0.1 broadcast_bitcast_fusion
  2.7 0.1 constant_dynamic-slice_fusion
  2.8 0.0 copy-start
  2.8 1.7 %copy-done = f32[2,10,1,128,256]{4,3,2,1,0:T(8,128)S(1)} copy-done((f32[2,10,1,128,256]{4,3,2,1,0:T(8,128)S(1)}, f32[2,10,1,128,256]{4,3,2,1,0:T(8,128)}, u32[]{:S(2)}) %copy-start) | copy-done | bytes 2621464
  4.5 0.0 copy-start.1
  4.5 129.7 %panel_product.1 = (f32[2,80,256]{2,1,0:T(8,128)S(1)}, f32[2,8,32,256]{3,2,1,0:T(8,128)S(1)}) custom-call(f32[2,10]{1,0:T(2,128)S(1)} %get-tuple-element.15.live_own, f32[2,10]{1,0:T(2,128)S(1)} %get-tuple-element.14.live_col, f32[12800,128]{1,0:T(8,128)} %bitcast.14, f32[2,10,128,256]{3,2,1,0:T(8,128)S(1)} %bitcast.13), custom_call_target="tpu_custom_call" | custom-call | tf_op jit(solution)/shard_map/panel_product/pallas_call | solution.py:304
  134.3 0.8 multiply_bitcast_fusion
  135.0 0.0 copy-done.1
  135.0 0.9 bitcast_add_fusion
  (2 shorter events, 0.0 us)
Async XLA Ops:
  2.8 1.7 %copy-start = (f32[2,10,1,128,256]{4,3,2,1,0:T(8,128)S(1)}, f32[2,10,1,128,256]{4,3,2,1,0:T(8,128)}, u32[]{:S(2)}) copy-start(f32[2,10,1,128,256]{4,3,2,1,0:T(8,128)} %param.6) | copy-start | bytes 7864324
  4.5 130.5 %copy-start.1 = (f32[2,256,256]{2,1,0:T(8,128)S(1)}, f32[2,256,256]{2,1,0:T(8,128)}, u32[]{:S(2)}) copy-start(f32[2,256,256]{2,1,0:T(8,128)} %param.9) | copy-start | bytes 1572868

commit v2 on v1

v2 whole, which is shorter than its diff:
```python
import functools

import jax
import jax.numpy as jnp
from jax import lax
from jax.experimental import pallas as pl
from jax.experimental.pallas import tpu as pltpu
from jax.sharding import PartitionSpec as P

MESH = pl.DeviceIdType.MESH
F32 = jnp.float32
BF16 = jnp.bfloat16

RING = 8
SUBS = 2
ROWS = 64 // SUBS
STEPS = 2 * 10 * SUBS
LAG = 8
TAIL = 2
SHARED = True


def split(value):
    high = value.astype(BF16)
    return high, (value - high.astype(F32)).astype(BF16)


def three_dots(a_high, a_low, b_high, b_low):
    dot = functools.partial(jnp.dot, preferred_element_type=F32)
    return dot(a_high, b_high) + (dot(a_high, b_low) + dot(a_low, b_high))


def kernel(
    live_own, live_col, a_hbm, panel_hbm,
    y_out, d_out,
    a_raw, a_high, a_low, own, own_high, own_low, x, x_high, x_low,
    y, y_peer, y_send, y_recv, d_part, d_peer, d_send, d_recv, d_pair, d_ring,
    load_sem, z_ssem, z_rsem, x_ssem, x_rsem, i_ssem, c_ssem, c_rsem, y_ssem, y_rsem, d_ssem, d_rsem, p_ssem, p_rsem,
    r_ssem, r_rsem, g_ssem, g_rsem,
):
    p = lax.axis_index("prow")
    q = lax.axis_index("pcol")
    half = p // RING
    z = p % RING
    place = q // 2
    core = q % 2
    root_half = q // RING
    hops = (z - q % RING + RING) % RING
    on_root = half == root_half

    across = ((1 - half) * RING + z, q)
    sibling = (p, place * 2 + 1 - core)

    def ring(step):
        return (half * RING + (z + step) % RING, q)

    def chip(step):
        return (p, ((place + step) % 8) * 2 + core)

    row_place = p // 2
    turn = (place // 2 - row_place // 2 + 5) % 4
    injects = (turn < 3) & (place % 2 != row_place % 2) & (core == p % 2)
    entry = ((1 - half) * RING + z, p)
    root = (root_half * RING + q % RING, q)

    def source(i):
        return (root[0], (((place // 2 + 3 + i) % 4) * 2 + 1 - place % 2) * 2 + core)

    load_own = pltpu.make_async_copy(panel_hbm, own, load_sem.at[0])
    load_own.start()
    load_root = pltpu.make_async_copy(panel_hbm, x, load_sem.at[1])

    @pl.when(p == q)
    def _():
        load_root.start()

    load_a = pltpu.make_async_copy(a_hbm, a_raw, load_sem.at[2])
    load_a.start()

    barrier = pltpu.get_barrier_semaphore()
    partners = [across, sibling] + [ring(i) for i in range(1, RING)] + [chip(i) for i in range(1, 8)]
    for partner in partners:
        pl.semaphore_signal(barrier, inc=1, device_id=partner, device_id_type=MESH)
    entered = (hops == 0) & jnp.logical_not(on_root)

    @pl.when(entered)
    def _():
        for i in range(3):
            pl.semaphore_signal(barrier, inc=1, device_id=source(i), device_id_type=MESH)

    @pl.when(injects)
    def _():
        pl.semaphore_signal(barrier, inc=1, device_id=entry, device_id_type=MESH)

    extra = jnp.where(entered, 3, 0) + jnp.where(injects, 1, 0)
    pl.semaphore_wait(barrier, len(partners) + extra)

    @pl.when(p == q)
    def _():
        load_root.wait()

    def chunk(way, s):
        block = s // SUBS
        row = way * 64 + (s % SUBS) * ROWS
        return x.at[block // 10, block % 10, pl.ds(row, ROWS)]

    def z_copy(way, s):
        return pltpu.make_async_remote_copy(
            src_ref=chunk(way, s), dst_ref=chunk(way, s), send_sem=z_ssem.at[way, s], recv_sem=z_rsem.at[way, s],
            device_id=ring(1 if way == 0 else RING - 1), device_id_type=MESH,
        )

    def x_copy(way, s):
        return pltpu.make_async_remote_copy(
            src_ref=chunk(way, s), dst_ref=chunk(way, s), send_sem=x_ssem.at[way, s], recv_sem=x_rsem.at[way, s],
            device_id=across, device_id_type=MESH,
        )

    def roles(way, s):
        if SHARED:
            kind = s % 3
            both = kind == 2
            carries = both | (on_root & (kind == 0)) | (jnp.logical_not(on_root) & (kind == 1))
        else:
            both = jnp.bool_(True)
            carries = jnp.bool_(True)
        done = hops if way == 0 else (RING - hops) % RING
        to_z = carries & (done < RING - 1)
        to_x = (hops != 0) & carries & jnp.logical_not(both)
        return carries, to_z, to_x

    def event(way, s):
        carries, to_z, to_x = roles(way, s)

        @pl.when((hops == 0) & jnp.logical_not(on_root))
        def _():
            x_copy(way, s).wait_recv()

        @pl.when((hops != 0) & carries)
        def _():
            z_copy(way, s).wait_recv()

        @pl.when(to_z)
        def _():
            z_copy(way, s).start()

        @pl.when(to_x)
        def _():
            x_copy(way, s).start()

    def i_copy(way, s):
        block = s // SUBS
        row = way * 64 + (s % SUBS) * ROWS
        src = own.at[block // 10, block % 10, pl.ds(row, ROWS)]
        return pltpu.make_async_remote_copy(
            src_ref=src, dst_ref=chunk(way, s), send_sem=i_ssem.at[way, s], recv_sem=x_rsem.at[way, s],
            device_id=entry, device_id_type=MESH,
        )

    def inject(s, carry):
        for way in range(2):

            @pl.when((2 * s + way) % 3 == turn)
            def _():
                i_copy(way, s).start()

        return carry

    load_own.wait()

    @pl.when(injects)
    def _():
        lax.fori_loop(0, STEPS, inject, 0)

    shift = jnp.where(hops == 0, 0, (RING - 2 * hops) * LAG)
    late_up = jnp.maximum(0, -shift)
    late_down = jnp.maximum(0, shift)

    def remote(src, dst, send, recv, device):
        return pltpu.make_async_remote_copy(
            src_ref=src, dst_ref=dst, send_sem=send, recv_sem=recv, device_id=device, device_id_type=MESH
        )

    def split_a(i):
        for col in range(10):
            high, low = split(a_raw[pl.ds(i * 640 + col, 64, stride=10), :])
            rows = pl.ds(pl.multiple_of(i * 64, 64), 64)
            a_high[rows, col * 128 : (col + 1) * 128] = high
            a_low[rows, col * 128 : (col + 1) * 128] = low

    def split_own(i):
        k, r = i // 10, i % 10
        rows = pl.ds(pl.multiple_of(r * 128, 128), 128)
        high, low = split((own[k, r] * live_own[k, r]).T)
        own_high[k, :, rows] = high
        own_low[k, :, rows] = low

    def arrived(s):
        for way in range(2):
            carries, _, _ = roles(way, s)

            @pl.when((hops != 0) & jnp.logical_not(carries))
            def _():
                x_copy(way, s).wait_recv()

    def take_block(k, r):
        if SHARED:
            for sub in range(SUBS):
                arrived((k * 10 + r) * SUBS + sub)
        rows = pl.ds(pl.multiple_of(r * 128, 128), 128)
        high, low = split(x[k, r] * live_col[k, r])
        x_high[rows] = high
        x_low[rows] = low

    def rows_of_y(k, m):
        rows = pl.ds(pl.multiple_of(m * 160, 32), 160)
        part = three_dots(a_high[rows], a_low[rows], x_high[...], x_low[...])
        y[k, m] = part.reshape(2, 80, 256)

    def terms(k):
        y_high, y_low = split(y[k].reshape(1280, 256))
        d_part[k] = three_dots(own_high[k], own_low[k], y_high, y_low).reshape(2, 8, 16, 256)

    def peer_d(k):
        return remote(d_part.at[k, 1 - core], d_peer.at[k], c_ssem.at[k, 0], c_rsem.at[k, 0], sibling)

    def peer_y(k):
        return remote(y.at[k, :, 1 - core], y_peer.at[k], c_ssem.at[k, 1], c_rsem.at[k, 1], sibling)

    def chip_d(k, step):
        to = (place + step) % 8
        return remote(d_send.at[k, to], d_recv.at[k, place], d_ssem.at[k, step], d_rsem.at[k, step], chip(step))

    def chip_y(k, step):
        to = (place + step) % 8
        return remote(y_send.at[k, to], y_recv.at[k, place], y_ssem.at[k, step], y_rsem.at[k, step], chip(step))

    def pair(k):
        return remote(d_pair.at[k, 0], d_pair.at[k, 1], p_ssem.at[k], p_rsem.at[k], across)

    def round_z(k, step):
        return remote(d_ring.at[k, z], d_ring.at[k, z], r_ssem.at[k, step], r_rsem.at[k, step], ring(step))

    def gather(k, step):
        mine = d_out.at[k, core, place]
        return remote(mine, mine, g_ssem.at[k, step], g_rsem.at[k, step], chip(step))

    def peer_out(k):
        mine = d_out.at[k, core]
        return remote(mine, mine, c_ssem.at[k, 2], c_rsem.at[k, 2], sibling)

    def to_sibling(k):
        peer_d(k).start()
        peer_y(k).start()

    def to_chips(k):
        peer_d(k).wait()
        for i in range(8):
            d_send[k, i] = d_part[k, core, i] + d_peer[k, i]
        for step in range(1, 8):
            chip_d(k, step).start()
        d_recv[k, place] = d_send[k, place]
        peer_y(k).wait()
        for i in range(8):
            y_send[k, i] = y[k, i, core] + y_peer[k, i]
        for step in range(1, 8):
            chip_y(k, step).start()
        y_recv[k, place] = y_send[k, place]

    def to_across(k):
        for step in range(1, 8):
            chip_d(k, step).wait()
        total = d_recv[k, 0]
        for i in range(1, 8):
            total = total + d_recv[k, i]
        d_pair[k, 0] = total
        pair(k).start()

    def to_ring(k):
        pair(k).wait()
        d_ring[k, z] = d_pair[k, 0] + d_pair[k, 1]
        for step in range(1, RING):
            round_z(k, step).start()

    def to_gather(k):
        for step in range(1, RING):
            round_z(k, step).wait()
        total = d_ring[k, 0]
        for i in range(1, RING):
            total = total + d_ring[k, i]
        d_out[k, core, place] = total
        for step in range(1, 8):
            gather(k, step).start()

    def to_out(k):
        for step in range(1, 8):
            gather(k, step).wait()
        peer_out(k).start()

    def sum_y(k):
        for step in range(1, 8):
            chip_y(k, step).wait()
        total = y_recv[k, 0]
        for i in range(1, 8):
            total = total + y_recv[k, i]
        y_out[k] = total

    load_a.wait()
    begin = jnp.where(hops == 0, STEPS, STEPS // 2 + jnp.maximum(late_up, late_down))

    def stream(t, carry):
        for way, late in ((0, late_up), (1, late_down)):
            s = t - late

            @pl.when((s >= 0) & (s < STEPS))
            def _():
                event(way, s)

        @pl.when(t < 20)
        def _():
            split_a(t)
            split_own(t)

        work = t - begin

        @pl.when((work >= 0) & (work < 5))
        def _():
            for i in range(2):
                take_block(0, work * 2 + i)

        @pl.when((work >= 5) & (work < 13))
        def _():
            rows_of_y(0, work - 5)

        @pl.when(work == 13)
        def _():
            terms(0)
            to_sibling(0)

        @pl.when(work == 20)
        def _():
            to_chips(0)

        return carry

    lax.fori_loop(0, STEPS + 6 * LAG + TAIL, stream, 0)

    def take(r, carry):
        take_block(1, r)
        return carry

    lax.fori_loop(0, 10, take, 0)
    to_across(0)

    def rows_of(m, carry):
        rows_of_y(1, m)
        return carry

    lax.fori_loop(0, 4, rows_of, 0)
    to_ring(0)
    lax.fori_loop(4, 8, rows_of, 0)
    terms(1)
    to_sibling(1)
    to_gather(0)
    to_chips(1)
    sum_y(0)
    to_across(1)
    to_out(0)
    to_ring(1)
    sum_y(1)
    to_gather(1)
    to_out(1)
    for k in range(2):
        peer_out(k).wait()

    def sent(s, carry):
        for way in range(2):
            _, to_z, to_x = roles(way, s)

            @pl.when(to_z)
            def _():
                z_copy(way, s).wait_send()

            @pl.when(to_x)
            def _():
                x_copy(way, s).wait_send()

            @pl.when(injects & ((2 * s + way) % 3 == turn))
            def _():
                i_copy(way, s).wait_send()

        return carry

    lax.fori_loop(0, STEPS, sent, 0)


def local(ancestor_inverse, factor_panel, structure, block_map, diag_inverse):
    row_count = lax.axis_size("prow")
    p = lax.axis_index("prow")
    q = lax.axis_index("pcol")
    blocks = block_map.shape[0]
    ids = jnp.arange(blocks, dtype=jnp.int32)
    in_structure = jnp.any(structure[:, :, None] == ids[None, None, :], axis=1)
    live = jnp.any(in_structure[:, :, None] & (block_map[None, :, None] == ids[None, None, :]), axis=1)
    live = live.astype(F32).reshape(2, 10, row_count)
    live_own = lax.dynamic_index_in_dim(live, p, 2, keepdims=False)
    live_col = lax.dynamic_index_in_dim(live, q, 2, keepdims=False)
    share_live = lax.dynamic_slice_in_dim(jnp.repeat(live_own, 128, axis=1), q * 80, 80, 1)

    dma = pltpu.SemaphoreType.DMA
    vmem = pltpu.VMEM
    columns, terms = pl.pallas_call(
        kernel,
        name="panel_product",
        out_shape=(jax.ShapeDtypeStruct((2, 80, 256), F32), jax.ShapeDtypeStruct((2, 2, 8, 16, 256), F32)),
        in_specs=[pl.BlockSpec(memory_space=pltpu.SMEM)] * 2 + [pl.BlockSpec(memory_space=pl.ANY)] * 2,
        out_specs=(pl.BlockSpec(memory_space=pltpu.VMEM),) * 2,
        scratch_shapes=[
            vmem((12800, 128), F32), vmem((1280, 1280), BF16), vmem((1280, 1280), BF16),
            vmem((2, 10, 128, 256), F32), vmem((2, 256, 1280), BF16), vmem((2, 256, 1280), BF16),
            vmem((2, 10, 128, 256), F32), vmem((1280, 256), BF16), vmem((1280, 256), BF16),
            vmem((2, 8, 2, 80, 256), F32), vmem((2, 8, 80, 256), F32), vmem((2, 8, 80, 256), F32),
            vmem((2, 8, 80, 256), F32),
            vmem((2, 2, 8, 16, 256), F32), vmem((2, 8, 16, 256), F32), vmem((2, 8, 16, 256), F32),
            vmem((2, 8, 16, 256), F32), vmem((2, 2, 16, 256), F32), vmem((2, RING, 16, 256), F32),
            dma((3,)), dma((2, STEPS)), dma((2, STEPS)), dma((2, STEPS)), dma((2, STEPS)), dma((2, STEPS)),
            dma((2, 3)), dma((2, 3)), dma((2, 8)), dma((2, 8)), dma((2, 8)), dma((2, 8)), dma((2,)), dma((2,)),
            dma((2, RING)), dma((2, RING)), dma((2, 8)), dma((2, 8)),
        ],
        compiler_params=pltpu.CompilerParams(collective_id=0, has_side_effects=True, vmem_limit_bytes=50 * 2**20),
    )(live_own, live_col, ancestor_inverse.reshape(12800, 128), factor_panel.reshape(2, 10, 128, 256))
    columns = -columns * share_live[:, :, None]
    return columns[:, None, None], diag_inverse + terms.reshape(2, 256, 256)


def solution(mesh):
    in_specs = (
        P(None, "prow", None, None, "pcol", None),
        P(None, None, "prow", None, None),
        P(),
        P(),
        P(),
    )
    out_specs = (P(None, "prow", "pcol", None, None), P())
    return jax.shard_map(local, mesh=mesh, in_specs=in_specs, out_specs=out_specs, check_vma=False)
```

time: 136 us -> 110 us (0.81)
  Pallas kernels: 130 us -> 103 us
    pallas_call x1, Pallas kernels: 130 us -> 103 us  [local(): pl.pallas_call(kernel, name='panel_product', out_shape=(jax.ShapeDtypeStr...]
where the time goes in v2:
time: 110 us
  Pallas kernels  103 us (94%)
  other arithmetic  3.35 us (3%)
  local copies, waits for them, and re-layouts  2.16 us (2%)
    pallas_call x1, Pallas kernels, local(): pl.pallas_call(kernel, name='panel_product', out_shape=(jax.ShapeDtypeStr...  103 us

profile of v2, /device:TPU:1, one launch (start us, length us, event | category | flops | bytes accessed | tf_op | source)
XLA Modules:
  0.0 109.5 jit_solution(17142964744005653336)
XLA Ops:
  0.6 0.8 fusion
  1.5 0.8 iota_compare_fusion
  2.2 0.1 and_reduce_fusion
  2.4 0.1 reshape.45
  2.5 0.2 dynamic-slice_reduce_fusion
  2.6 0.1 broadcast_bitcast_fusion
  2.7 0.1 constant_dynamic-slice_fusion
  2.8 0.0 copy-start
  2.8 1.7 %copy-done = f32[2,10,1,128,256]{4,3,2,1,0:T(8,128)S(1)} copy-done((f32[2,10,1,128,256]{4,3,2,1,0:T(8,128)S(1)}, f32[2,10,1,128,256]{4,3,2,1,0:T(8,128)}, u32[]{:S(2)}) %copy-start) | copy-done | bytes 2621464
  4.5 0.0 copy-start.1
  4.5 103.3 %panel_product.1 = (f32[2,80,256]{2,1,0:T(8,128)S(1)}, f32[2,2,8,16,256]{4,3,2,1,0:T(8,128)S(1)}) custom-call(f32[2,10]{1,0:T(2,128)S(1)} %get-tuple-element.15.live_own, f32[2,10]{1,0:T(2,128)S(1)} %get-tuple-element.14.live_col, f32[12800,128]{1,0:T(8,128)} %bitcast.14, f32[2,10,128,256]{3,2,1,0:T(8,128)S(1)} %bitcast.13), custom_call_target="tpu_custom_call" | custom-call | tf_op jit(solution)/shard_map/panel_product/pallas_call | solution.py:412
  107.9 0.8 multiply_bitcast_fusion
  108.6 0.0 copy-done.1
  108.6 0.9 bitcast_add_fusion
  (2 shorter events, 0.0 us)
Async XLA Ops:
  2.8 1.7 %copy-start = (f32[2,10,1,128,256]{4,3,2,1,0:T(8,128)S(1)}, f32[2,10,1,128,256]{4,3,2,1,0:T(8,128)}, u32[]{:S(2)}) copy-start(f32[2,10,1,128,256]{4,3,2,1,0:T(8,128)} %param.6) | copy-start | bytes 7864324
  4.5 104.1 %copy-start.1 = (f32[2,256,256]{2,1,0:T(8,128)S(1)}, f32[2,256,256]{2,1,0:T(8,128)}, u32[]{:S(2)}) copy-start(f32[2,256,256]{2,1,0:T(8,128)} %param.9) | copy-start | bytes 1572868

commit v3 on v2

v3 whole, which is shorter than its diff:
```python
import functools

import jax
import jax.numpy as jnp
from jax import lax
from jax.experimental import pallas as pl
from jax.experimental.pallas import tpu as pltpu
from jax.sharding import PartitionSpec as P

MESH = pl.DeviceIdType.MESH
F32 = jnp.float32
BF16 = jnp.bfloat16

RING = 8
SUBS = 2
ROWS = 64 // SUBS
STEPS = 2 * 10 * SUBS
PERIOD = 2
APART = 12
LEAD = 8
SLACK = 4
HALF = STEPS // 2


def split(value):
    high = value.astype(BF16)
    return high, (value - high.astype(F32)).astype(BF16)


def three_dots(a_high, a_low, b_high, b_low):
    dot = functools.partial(jnp.dot, preferred_element_type=F32)
    return dot(a_high, b_high) + (dot(a_high, b_low) + dot(a_low, b_high))


def kernel(
    live_own, live_col, a_hbm, panel_hbm,
    y_out, d_out,
    a_raw, a_high, a_low, own, own_high, own_low, u_high, u_low, x, x_high, x_low,
    y, y_peer, y_send, y_recv, d_part, d_peer, d_send, d_recv, d_ring,
    load_sem, z_ssem, z_rsem, x_ssem, x_rsem, i_ssem, c_ssem, c_rsem, y_ssem, y_rsem, d_ssem, d_rsem,
    r_ssem, r_rsem, g_ssem, g_rsem, m_ssem, m_rsem,
):
    p = lax.axis_index("prow")
    q = lax.axis_index("pcol")
    half = p // RING
    z = p % RING
    place = q // 2
    core = q % 2
    root_half = q // RING
    hops = (z - q % RING + RING) % RING
    on_root = half == root_half

    spot = half * 8 + place
    across = ((1 - half) * RING + z, q)
    sibling = (p, place * 2 + 1 - core)

    def ring(step):
        return (half * RING + (z + step) % RING, q)

    def chip(step):
        return (p, ((place + step) % 8) * 2 + core)

    def plane(step):
        to = (spot + step) % 16
        return ((to // 8) * RING + z, (to % 8) * 2 + core)

    row_place = p // 2
    turn = (place // 2 - row_place // 2 + 4) % 4
    injects = (place % 2 != row_place % 2) & (core == p % 2)
    entry = ((1 - half) * RING + z, p)
    root = (root_half * RING + q % RING, q)

    def source(i):
        return (root[0], (((place // 2 + i) % 4) * 2 + 1 - place % 2) * 2 + core)

    load_own = pltpu.make_async_copy(panel_hbm, own, load_sem.at[0])
    load_own.start()
    load_root = pltpu.make_async_copy(panel_hbm, x, load_sem.at[1])

    @pl.when(p == q)
    def _():
        load_root.start()

    load_a = pltpu.make_async_copy(a_hbm, a_raw, load_sem.at[2])
    load_a.start()

    barrier = pltpu.get_barrier_semaphore()
    partners = [sibling] + [ring(i) for i in range(1, RING)] + [plane(i) for i in range(1, 16)]
    for partner in partners:
        pl.semaphore_signal(barrier, inc=1, device_id=partner, device_id_type=MESH)
    entered = (hops == 0) & jnp.logical_not(on_root)

    @pl.when(entered)
    def _():
        for i in range(4):
            pl.semaphore_signal(barrier, inc=1, device_id=source(i), device_id_type=MESH)

    @pl.when(injects)
    def _():
        pl.semaphore_signal(barrier, inc=1, device_id=entry, device_id_type=MESH)

    extra = jnp.where(entered, 4, 0) + jnp.where(injects, 1, 0)
    pl.semaphore_wait(barrier, len(partners) + extra)

    @pl.when(p == q)
    def _():
        load_root.wait()

    def rows_of_chunk(way, s):
        row = lax.div(s, SUBS) * 128 + way * 64 + lax.rem(s, SUBS) * ROWS
        return pl.ds(pl.multiple_of(row, ROWS), ROWS)

    def chunk(way, s):
        return x.at[rows_of_chunk(way, s)]

    def z_copy(way, s, step):
        return pltpu.make_async_remote_copy(
            src_ref=chunk(way, s), dst_ref=chunk(way, s), send_sem=z_ssem.at[min(step - 1, 1), way, s],
            recv_sem=z_rsem.at[way, s], device_id=ring(step), device_id_type=MESH,
        )

    def x_copy(way, s):
        return pltpu.make_async_remote_copy(
            src_ref=chunk(way, s), dst_ref=chunk(way, s), send_sem=x_ssem.at[way, s], recv_sem=x_rsem.at[way, s],
            device_id=across, device_id_type=MESH,
        )

    def roles(way, s):
        kind = lax.rem(s, PERIOD)
        both = kind >= 2
        carries = both | (kind == jnp.where(on_root, 0, 1))
        up = carries & (hops < RING // 2)
        down = carries & ((hops == 0) | (hops > RING // 2 + 1))
        to_x = (hops != 0) & carries & jnp.logical_not(both)
        return carries, up, down, to_x

    def event(way, s):
        carries, up, down, to_x = roles(way, s)

        @pl.when((hops == 0) & jnp.logical_not(on_root))
        def _():
            x_copy(way, s).wait_recv()

        @pl.when((hops != 0) & carries)
        def _():
            z_copy(way, s, 1).wait_recv()

        @pl.when(up)
        def _():
            z_copy(way, s, 1).start()

        @pl.when(down)
        def _():
            z_copy(way, s, RING - 1).start()

        @pl.when(to_x)
        def _():
            x_copy(way, s).start()

    def i_copy(way, s):
        src = own.at[rows_of_chunk(way, s)]
        return pltpu.make_async_remote_copy(
            src_ref=src, dst_ref=chunk(way, s), send_sem=i_ssem.at[way, s], recv_sem=x_rsem.at[way, s],
            device_id=entry, device_id_type=MESH,
        )

    def entry_copy(j):
        way = lax.rem(turn, 2)
        return i_copy(way, 2 * j + lax.div(turn, 2))

    def inject(j, carry):
        entry_copy(j).start()
        return carry

    load_own.wait()

    @pl.when(injects)
    def _():
        lax.fori_loop(0, LEAD, inject, 0)

    def remote(src, dst, send, recv, device):
        return pltpu.make_async_remote_copy(
            src_ref=src, dst_ref=dst, send_sem=send, recv_sem=recv, device_id=device, device_id_type=MESH
        )

    def split_a(i):
        for col in range(10):
            high, low = split(a_raw[pl.ds(i * 640 + col, 64, stride=10), :])
            rows = pl.ds(pl.multiple_of(i * 64, 64), 64)
            a_high[rows, col * 128 : (col + 1) * 128] = high
            a_low[rows, col * 128 : (col + 1) * 128] = low

    def split_own(i):
        k, r = lax.div(i, 10), lax.rem(i, 10)
        rows = pl.ds(pl.multiple_of(r * 128, 128), 128)
        high, low = split((own[pl.ds(pl.multiple_of(i * 128, 128), 128)] * live_own[k, r]).T)
        own_high[k, :, rows] = high
        own_low[k, :, rows] = low

    def arrived(s):
        for way in range(2):
            carries, _, _, _ = roles(way, s)

            @pl.when((hops != 0) & jnp.logical_not(carries))
            def _():
                x_copy(way, s).wait_recv()

    def take_block(k, r):
        for sub in range(SUBS):
            arrived((k * 10 + r) * SUBS + sub)
        rows = pl.ds(pl.multiple_of(r * 128, 128), 128)
        high, low = split(x[pl.ds(pl.multiple_of((k * 10 + r) * 128, 128), 128)] * live_col[k, r])
        x_high[k, rows] = high
        x_low[k, rows] = low

    def rows_of_y(k, m):
        rows = pl.ds(pl.multiple_of(m * 160, 32), 160)
        part = three_dots(a_high[rows], a_low[rows], x_high[k], x_low[k])
        y[k, m] = part.reshape(2, 80, 256)

    def left_product(i):
        k = lax.div(i, 5)
        cols = pl.ds(pl.multiple_of(lax.rem(i, 5) * 256, 256), 256)
        high, low = split(three_dots(own_high[k], own_low[k], a_high[:, cols], a_low[:, cols]))
        u_high[k, :, cols] = high
        u_low[k, :, cols] = low

    def terms(k):
        d_part[k] = three_dots(u_high[k], u_low[k], x_high[k], x_low[k]).reshape(2, 16, 8, 256)
        peer_d(k).start()

    def peer_d(k):
        return remote(d_part.at[k, 1 - core], d_peer.at[k], c_ssem.at[k, 0], c_rsem.at[k, 0], sibling)

    def peer_rows(k, i):
        m = lax.rem(place + 1 + i, 8)
        return remote(y.at[k, m, 1 - core], y_peer.at[k, m], m_ssem.at[k, i], m_rsem.at[k, i], sibling)

    def rows_to_peer(k, i):
        rows_of_y(k, lax.rem(place + 1 + i, 8))
        peer_rows(k, i).start()

    def rows_to_chip(k, i):
        m = lax.rem(place + 1 + i, 8)
        peer_rows(k, i).wait()
        y_send[k, m] = y[k, m, core] + y_peer[k, m]

        @pl.when(i < 7)
        def _():
            chip_y(k, i + 1).start()

        @pl.when(i == 7)
        def _():
            y_recv[k, place] = y_send[k, place]

    def plane_d(k, step):
        to = (spot + step) % 16
        return remote(d_send.at[k, to], d_recv.at[k, spot], d_ssem.at[k, step], d_rsem.at[k, step], plane(step))

    def chip_y(k, step):
        to = (place + step) % 8
        return remote(y_send.at[k, to], y_recv.at[k, place], y_ssem.at[k, step], y_rsem.at[k, step], chip(step))

    def round_z(step):
        return remote(d_ring.at[z], d_ring.at[z], r_ssem.at[step], r_rsem.at[step], ring(step))

    def gather(step):
        mine = d_out.at[:, core, spot]
        return remote(mine, mine, g_ssem.at[step], g_rsem.at[step], plane(step))

    def peer_out():
        mine = d_out.at[:, core]
        return remote(mine, mine, c_ssem.at[0, 2], c_rsem.at[0, 2], sibling)

    def d_to_plane(k):
        peer_d(k).wait()
        d_send[k] = d_part[k, core] + d_peer[k]
        for step in range(1, 16):
            plane_d(k, step).start()
        d_recv[k, spot] = d_send[k, spot]

    def d_to_ring():
        for k in range(2):
            for step in range(1, 16):
                plane_d(k, step).wait()
            total = d_recv[k, 0]
            for i in range(1, 16):
                total = total + d_recv[k, i]
            d_ring[z, k] = total
        for step in range(1, RING):
            round_z(step).start()

    def d_to_gather():
        for step in range(1, RING):
            round_z(step).wait()
        for k in range(2):
            total = d_ring[0, k]
            for i in range(1, RING):
                total = total + d_ring[i, k]
            d_out[k, core, spot] = total
        for step in range(1, 16):
            gather(step).start()

    def sum_y(k):
        for step in range(1, 8):
            chip_y(k, step).wait()
        total = y_recv[k, 0]
        for i in range(1, 8):
            total = total + y_recv[k, i]
        y_out[k] = total

    load_a.wait()
    begin = jnp.where(hops == 0, STEPS, max(HALF, 26))
    begin_last = HALF + SUBS + SLACK

    def stream(t, carry):
        @pl.when(t < STEPS)
        def _():
            event(0, t)
            event(1, t)

        @pl.when(injects & (t < STEPS // 2 - LEAD))
        def _():
            entry_copy(t + LEAD).start()

        @pl.when(t < 20)
        def _():
            split_a(t)
            split_own(t)

        work = t - begin

        @pl.when((work >= 0) & (work < 5))
        def _():
            for i in range(2):
                take_block(0, work * 2 + i)

        @pl.when(work == 5)
        def _():
            terms(0)

        @pl.when((work >= 6) & (work < 14))
        def _():
            rows_to_peer(0, work - 6)

        @pl.when((work >= 6 + APART) & (work < 14 + APART))
        def _():
            rows_to_chip(0, work - 6 - APART)

        @pl.when(work == 5 + APART)
        def _():
            d_to_plane(0)

        @pl.when((t >= 20) & (t < 30))
        def _():
            left_product(t - 20)

        block = lax.div(t - begin_last, SUBS)

        @pl.when((t >= begin_last) & (block < 10) & (lax.rem(t - begin_last, SUBS) == 0))
        def _():
            take_block(1, block)

        return carry

    lax.fori_loop(0, STEPS + 14 + APART, stream, 0)

    terms(1)

    def last_rows(i, carry):
        @pl.when(i < 8)
        def _():
            rows_to_peer(1, i)

        @pl.when(i == 1)
        def _():
            d_to_plane(1)

        @pl.when(i >= 2)
        def _():
            rows_to_chip(1, i - 2)

        @pl.when(i == 6)
        def _():
            d_to_ring()

        return carry

    lax.fori_loop(0, 10, last_rows, 0)
    sum_y(0)
    def sent(s, carry):
        for way in range(2):
            _, up, down, to_x = roles(way, s)

            @pl.when(up)
            def _():
                z_copy(way, s, 1).wait_send()

            @pl.when(down)
            def _():
                z_copy(way, s, RING - 1).wait_send()

            @pl.when(to_x)
            def _():
                x_copy(way, s).wait_send()

        return carry

    lax.fori_loop(0, STEPS, sent, 0)

    def entered_all(j, carry):
        entry_copy(j).wait_send()
        return carry

    @pl.when(injects)
    def _():
        lax.fori_loop(0, STEPS // 2, entered_all, 0)

    d_to_gather()
    sum_y(1)
    for step in range(1, 16):
        gather(step).wait()
    peer_out().start()
    peer_out().wait()


def local(ancestor_inverse, factor_panel, structure, block_map, diag_inverse):
    row_count = lax.axis_size("prow")
    p = lax.axis_index("prow")
    q = lax.axis_index("pcol")
    blocks = block_map.shape[0]
    ids = jnp.arange(blocks, dtype=jnp.int32)
    in_structure = jnp.any(structure[:, :, None] == ids[None, None, :], axis=1)
    live = jnp.any(in_structure[:, :, None] & (block_map[None, :, None] == ids[None, None, :]), axis=1)
    live = live.astype(F32).reshape(2, 10, row_count)
    live_own = lax.dynamic_index_in_dim(live, p, 2, keepdims=False)
    live_col = lax.dynamic_index_in_dim(live, q, 2, keepdims=False)
    share_live = lax.dynamic_slice_in_dim(jnp.repeat(live_own, 128, axis=1), q * 80, 80, 1)

    dma = pltpu.SemaphoreType.DMA
    vmem = pltpu.VMEM
    columns, terms = pl.pallas_call(
        kernel,
        name="panel_product",
        out_shape=(jax.ShapeDtypeStruct((2, 80, 256), F32), jax.ShapeDtypeStruct((2, 2, 16, 8, 256), F32)),
        in_specs=[pl.BlockSpec(memory_space=pltpu.SMEM)] * 2 + [pl.BlockSpec(memory_space=pl.ANY)] * 2,
        out_specs=(pl.BlockSpec(memory_space=pltpu.VMEM),) * 2,
        scratch_shapes=[
            vmem((12800, 128), F32), vmem((1280, 1280), BF16), vmem((1280, 1280), BF16),
            vmem((2560, 256), F32), vmem((2, 256, 1280), BF16), vmem((2, 256, 1280), BF16),
            vmem((2, 256, 1280), BF16), vmem((2, 256, 1280), BF16),
            vmem((2560, 256), F32), vmem((2, 1280, 256), BF16), vmem((2, 1280, 256), BF16),
            vmem((2, 8, 2, 80, 256), F32), vmem((2, 8, 80, 256), F32), vmem((2, 8, 80, 256), F32),
            vmem((2, 8, 80, 256), F32),
            vmem((2, 2, 16, 8, 256), F32), vmem((2, 16, 8, 256), F32), vmem((2, 16, 8, 256), F32),
            vmem((2, 16, 8, 256), F32), vmem((RING, 2, 8, 256), F32),
            dma((3,)), dma((2, 2, STEPS)), dma((2, STEPS)), dma((2, STEPS)), dma((2, STEPS)), dma((2, STEPS)),
            dma((2, 3)), dma((2, 3)), dma((2, 8)), dma((2, 8)), dma((2, 16)), dma((2, 16)),
            dma((RING,)), dma((RING,)), dma((16,)), dma((16,)), dma((2, 8)), dma((2, 8)),
        ],
        compiler_params=pltpu.CompilerParams(collective_id=0, has_side_effects=True, vmem_limit_bytes=50 * 2**20),
    )(live_own, live_col, ancestor_inverse.reshape(12800, 128), factor_panel.reshape(2560, 256))
    columns = -columns * share_live[:, :, None]
    return columns[:, None, None], diag_inverse + terms.reshape(2, 256, 256)


def solution(mesh):
    in_specs = (
        P(None, "prow", None, None, "pcol", None),
        P(None, None, "prow", None, None),
        P(),
        P(),
        P(),
    )
    out_specs = (P(None, "prow", "pcol", None, None), P())
    return jax.shard_map(local, mesh=mesh, in_specs=in_specs, out_specs=out_specs, check_vma=False)
```

time: 110 us -> 99.1 us (0.901)
  Pallas kernels: 103 us -> 92.8 us
    pallas_call x1, Pallas kernels: 103 us -> 92.8 us  [local(): pl.pallas_call(kernel, name='panel_product', out_shape=(jax.ShapeDtypeStr...]
where the time goes in v3:
time: 99.1 us; the launch traced here: 98.9 us
  Pallas kernels  92.8 us (94%)
  other arithmetic  3.35 us (3%)
  local copies, waits for them, and re-layouts  2.16 us (2%)
    pallas_call x1, Pallas kernels, local(): pl.pallas_call(kernel, name='panel_product', out_shape=(jax.ShapeDtypeStr...  92.8 us

profile of v3, /device:TPU:1, one launch (start us, length us, event | category | flops | bytes accessed | tf_op | source)
XLA Modules:
  0.0 98.9 jit_solution(9317004035461444466)
XLA Ops:
  0.6 0.8 fusion
  1.5 0.8 iota_compare_fusion
  2.2 0.1 and_reduce_fusion
  2.4 0.1 reshape.45
  2.5 0.2 dynamic-slice_reduce_fusion
  2.6 0.1 broadcast_bitcast_fusion
  2.7 0.1 constant_dynamic-slice_fusion
  2.8 0.0 copy-start
  2.8 1.7 %copy-done = f32[2,10,1,128,256]{4,3,2,1,0:T(8,128)S(1)} copy-done((f32[2,10,1,128,256]{4,3,2,1,0:T(8,128)S(1)}, f32[2,10,1,128,256]{4,3,2,1,0:T(8,128)}, u32[]{:S(2)}) %copy-start) | copy-done | bytes 2621464
  4.5 0.0 copy-start.1
  4.5 92.8 %panel_product.1 = (f32[2,80,256]{2,1,0:T(8,128)S(1)}, f32[2,2,16,8,256]{4,3,2,1,0:T(8,128)S(1)}) custom-call(f32[2,10]{1,0:T(2,128)S(1)} %get-tuple-element.15.live_own, f32[2,10]{1,0:T(2,128)S(1)} %get-tuple-element.14.live_col, f32[12800,128]{1,0:T(8,128)} %bitcast.14, f32[2560,256]{1,0:T(8,128)S(1)} %bitcast.13), custom_call_target="tpu_custom_call" | custom-call | tf_op jit(solution)/shard_map/panel_product/pallas_call | solution.py:442
  97.3 0.8 multiply_bitcast_fusion
  98.1 0.0 copy-done.1
  98.1 0.9 bitcast_add_fusion
  (2 shorter events, 0.0 us)
Async XLA Ops:
  2.8 1.7 %copy-start = (f32[2,10,1,128,256]{4,3,2,1,0:T(8,128)S(1)}, f32[2,10,1,128,256]{4,3,2,1,0:T(8,128)}, u32[]{:S(2)}) copy-start(f32[2,10,1,128,256]{4,3,2,1,0:T(8,128)} %param.6) | copy-start | bytes 7864324
  4.5 93.5 %copy-start.1 = (f32[2,256,256]{2,1,0:T(8,128)S(1)}, f32[2,256,256]{2,1,0:T(8,128)}, u32[]{:S(2)}) copy-start(f32[2,256,256]{2,1,0:T(8,128)} %param.9) | copy-start | bytes 1572868

commit v4 on v3

--- a/solution.py
+++ b/solution.py
@@ -33,9 +33,9 @@
 
 
 def kernel(
-    live_own, live_col, a_hbm, panel_hbm,
+    structure, block_map, a_hbm, panel_hbm,
     y_out, d_out,
-    a_raw, a_high, a_low, own, own_high, own_low, u_high, u_low, x, x_high, x_low,
+    live_own, live_col, a_raw, a_high, a_low, own, own_high, own_low, u_high, u_low, x, x_high, x_low,
     y, y_peer, y_send, y_recv, d_part, d_peer, d_send, d_recv, d_ring,
     load_sem, z_ssem, z_rsem, x_ssem, x_rsem, i_ssem, c_ssem, c_rsem, y_ssem, y_rsem, d_ssem, d_rsem,
     r_ssem, r_rsem, g_ssem, g_rsem, m_ssem, m_rsem,
@@ -99,6 +99,18 @@
     def _():
         pl.semaphore_signal(barrier, inc=1, device_id=entry, device_id_type=MESH)
 
+    lanes = lax.broadcasted_iota(jnp.int32, (1, 256), 1)
+
+    def mark(b, live):
+        return tuple(jnp.where(lanes == block_map[structure[k, b]], 1.0, live[k]) for k in range(2))
+
+    live = lax.fori_loop(0, 120, mark, (jnp.zeros((1, 256), F32),) * 2)
+    for k in range(2):
+        for r in range(10):
+            for ref, index in ((live_own, p), (live_col, q)):
+                found = jnp.sum(jnp.where(lanes == r * 16 + index, live[k], 0.0), axis=1, keepdims=True)
+                ref[k * 10 + r] = jnp.broadcast_to(found, (8, 256))
+
     extra = jnp.where(entered, 4, 0) + jnp.where(injects, 1, 0)
     pl.semaphore_wait(barrier, len(partners) + extra)
 
@@ -126,7 +138,7 @@
         )
 
     def roles(way, s):
-        kind = lax.rem(s, PERIOD)
+        kind = jnp.where(lax.rem(s, 8) == 7, 2, lax.rem(s, PERIOD))
         both = kind >= 2
         carries = both | (kind == jnp.where(on_root, 0, 1))
         up = carries & (hops < RING // 2)
@@ -193,7 +205,7 @@
     def split_own(i):
         k, r = lax.div(i, 10), lax.rem(i, 10)
         rows = pl.ds(pl.multiple_of(r * 128, 128), 128)
-        high, low = split((own[pl.ds(pl.multiple_of(i * 128, 128), 128)] * live_own[k, r]).T)
+        high, low = split((own[pl.ds(pl.multiple_of(i * 128, 128), 128)] * live_own[i, 0:1]).T)
         own_high[k, :, rows] = high
         own_low[k, :, rows] = low
 
@@ -209,7 +221,7 @@
         for sub in range(SUBS):
             arrived((k * 10 + r) * SUBS + sub)
         rows = pl.ds(pl.multiple_of(r * 128, 128), 128)
-        high, low = split(x[pl.ds(pl.multiple_of((k * 10 + r) * 128, 128), 128)] * live_col[k, r])
+        high, low = split(x[pl.ds(pl.multiple_of((k * 10 + r) * 128, 128), 128)] * live_col[k * 10 + r, 0:1])
         x_high[k, rows] = high
         x_low[k, rows] = low
 
@@ -307,7 +319,10 @@
         total = y_recv[k, 0]
         for i in range(1, 8):
             total = total + y_recv[k, i]
-        y_out[k] = total
+        slot = lax.div(q * 80, 128)
+        rows = q * 80 + lax.broadcasted_iota(jnp.int32, (80, 256), 0)
+        after = live_own[k * 10 + jnp.minimum(slot + 1, 9), 0:1]
+        y_out[k] = -total * jnp.where(rows < slot * 128 + 128, live_own[k * 10 + slot, 0:1], after)
 
     load_a.wait()
     begin = jnp.where(hops == 0, STEPS, max(HALF, 26))
@@ -425,18 +440,6 @@
 
 
 def local(ancestor_inverse, factor_panel, structure, block_map, diag_inverse):
-    row_count = lax.axis_size("prow")
-    p = lax.axis_index("prow")
-    q = lax.axis_index("pcol")
-    blocks = block_map.shape[0]
-    ids = jnp.arange(blocks, dtype=jnp.int32)
-    in_structure = jnp.any(structure[:, :, None] == ids[None, None, :], axis=1)
-    live = jnp.any(in_structure[:, :, None] & (block_map[None, :, None] == ids[None, None, :]), axis=1)
-    live = live.astype(F32).reshape(2, 10, row_count)
-    live_own = lax.dynamic_index_in_dim(live, p, 2, keepdims=False)
-    live_col = lax.dynamic_index_in_dim(live, q, 2, keepdims=False)
-    share_live = lax.dynamic_slice_in_dim(jnp.repeat(live_own, 128, axis=1), q * 80, 80, 1)
-
     dma = pltpu.SemaphoreType.DMA
     vmem = pltpu.VMEM
     columns, terms = pl.pallas_call(
@@ -446,7 +449,7 @@
         in_specs=[pl.BlockSpec(memory_space=pltpu.SMEM)] * 2 + [pl.BlockSpec(memory_space=pl.ANY)] * 2,
         out_specs=(pl.BlockSpec(memory_space=pltpu.VMEM),) * 2,
         scratch_shapes=[
-            vmem((12800, 128), F32), vmem((1280, 1280), BF16), vmem((1280, 1280), BF16),
+            vmem((20, 8, 256), F32), vmem((20, 8, 256), F32), vmem((12800, 128), F32), vmem((1280, 1280), BF16), vmem((1280, 1280), BF16),
             vmem((2560, 256), F32), vmem((2, 256, 1280), BF16), vmem((2, 256, 1280), BF16),
             vmem((2, 256, 1280), BF16), vmem((2, 256, 1280), BF16),
             vmem((2560, 256), F32), vmem((2, 1280, 256), BF16), vmem((2, 1280, 256), BF16),
@@ -459,8 +462,7 @@
             dma((RING,)), dma((RING,)), dma((16,)), dma((16,)), dma((2, 8)), dma((2, 8)),
         ],
         compiler_params=pltpu.CompilerParams(collective_id=0, has_side_effects=True, vmem_limit_bytes=50 * 2**20),
-    )(live_own, live_col, ancestor_inverse.reshape(12800, 128), factor_panel.reshape(2560, 256))
-    columns = -columns * share_live[:, :, None]
+    )(structure, block_map, ancestor_inverse.reshape(12800, 128), factor_panel.reshape(2560, 256))
     return columns[:, None, None], diag_inverse + terms.reshape(2, 256, 256)
 
 

time: 99.1 us -> 96.3 us (0.972)
  other arithmetic: 3.35 us -> 0.86 us
  Pallas kernels: 92.8 us -> 90.9 us
  local copies, waits for them, and re-layouts: 2.16 us -> 3.76 us
    unnamed x6 -> x9, local copies, waits for them, and re-layouts: 1.83 us -> 3.76 us
    pallas_call x1, Pallas kernels: 92.8 us -> 90.9 us  [local(): pl.pallas_call(kernel, name='panel_product', out_shape=(jax.ShapeDtypeStr...]
where the time goes in v4:
time: 96.3 us; the launch traced here: 96.2 us
  Pallas kernels  90.9 us (94%)
  local copies, waits for them, and re-layouts  3.76 us (4%)
    pallas_call x1, Pallas kernels, local(): pl.pallas_call(kernel, name='panel_product', out_shape=(jax.ShapeDtypeStr...  90.9 us
    unnamed x9, local copies, waits for them, and re-layouts  3.76 us

profile of v4, /device:TPU:1, one launch (start us, length us, event | category | flops | bytes accessed | tf_op | source)
XLA Modules:
  0.0 96.2 jit_solution(8316664586690039690)
XLA Ops:
  0.6 0.0 copy-start
  0.6 1.7 %copy-done = f32[2,10,1,128,256]{4,3,2,1,0:T(8,128)S(1)} copy-done((f32[2,10,1,128,256]{4,3,2,1,0:T(8,128)S(1)}, f32[2,10,1,128,256]{4,3,2,1,0:T(8,128)}, u32[]{:S(2)}) %copy-start) | copy-done | bytes 2621464
  2.4 0.0 copy-start.1
  2.4 0.7 copy-done.1
  3.1 0.0 copy-start.2
  3.1 0.7 copy-done.2
  3.7 0.0 copy-start.3
  3.7 90.9 %panel_product.1 = (f32[2,80,256]{2,1,0:T(8,128)S(1)}, f32[2,2,16,8,256]{4,3,2,1,0:T(8,128)S(1)}) custom-call(s32[2,120]{1,0:T(2,128)S(1)} %copy-done.1, s32[160]{0:T(256)S(1)} %copy-done.2, f32[12800,128]{1,0:T(8,128)} %bitcast.9, f32[2560,256]{1,0:T(8,128)S(1)} %bitcast.7), custom_call_target="tpu_custom_call" | custom-call | tf_op jit(solution)/shard_map/panel_product/pallas_call | solution.py:445
  94.6 0.0 copy-done.3
  94.6 0.9 bitcast_add_fusion
  95.5 0.7 copy.9
Async XLA Ops:
  0.6 1.7 %copy-start = (f32[2,10,1,128,256]{4,3,2,1,0:T(8,128)S(1)}, f32[2,10,1,128,256]{4,3,2,1,0:T(8,128)}, u32[]{:S(2)}) copy-start(f32[2,10,1,128,256]{4,3,2,1,0:T(8,128)} %param.6) | copy-start | bytes 7864324
  2.4 0.7 copy-start.1
  3.1 0.7 copy-start.2
  3.7 90.9 %copy-start.3 = (f32[2,256,256]{2,1,0:T(8,128)S(1)}, f32[2,256,256]{2,1,0:T(8,128)}, u32[]{:S(2)}) copy-start(f32[2,256,256]{2,1,0:T(8,128)} %param.9) | copy-start | bytes 1572868

commit v5 on v4

--- a/solution.py
+++ b/solution.py
@@ -16,7 +16,7 @@
 ROWS = 64 // SUBS
 STEPS = 2 * 10 * SUBS
 PERIOD = 2
-APART = 12
+APART = 16
 LEAD = 8
 SLACK = 4
 HALF = STEPS // 2

time: 96.3 us -> 96.9 us (level)
  no operation moved by 1% of the time
where the time goes in v5:
time: 96.9 us; the launch traced here: 96.7 us
  Pallas kernels  91.5 us (94%)
  local copies, waits for them, and re-layouts  3.76 us (4%)
    pallas_call x1, Pallas kernels, local(): pl.pallas_call(kernel, name='panel_product', out_shape=(jax.ShapeDtypeStr...  91.5 us
    unnamed x9, local copies, waits for them, and re-layouts  3.76 us

profile of v5, /device:TPU:1, one launch (start us, length us, event | category | flops | bytes accessed | tf_op | source)
XLA Modules:
  0.0 96.7 jit_solution(13626449995722452473)
XLA Ops:
  0.6 0.0 copy-start
  0.6 1.7 %copy-done = f32[2,10,1,128,256]{4,3,2,1,0:T(8,128)S(1)} copy-done((f32[2,10,1,128,256]{4,3,2,1,0:T(8,128)S(1)}, f32[2,10,1,128,256]{4,3,2,1,0:T(8,128)}, u32[]{:S(2)}) %copy-start) | copy-done | bytes 2621464
  2.4 0.0 copy-start.1
  2.4 0.7 copy-done.1
  3.1 0.0 copy-start.2
  3.1 0.7 copy-done.2
  3.7 0.0 copy-start.3
  3.7 91.5 %panel_product.1 = (f32[2,80,256]{2,1,0:T(8,128)S(1)}, f32[2,2,16,8,256]{4,3,2,1,0:T(8,128)S(1)}) custom-call(s32[2,120]{1,0:T(2,128)S(1)} %copy-done.1, s32[160]{0:T(256)S(1)} %copy-done.2, f32[12800,128]{1,0:T(8,128)} %bitcast.9, f32[2560,256]{1,0:T(8,128)S(1)} %bitcast.7), custom_call_target="tpu_custom_call" | custom-call | tf_op jit(solution)/shard_map/panel_product/pallas_call | solution.py:445
  95.2 0.0 copy-done.3
  95.2 0.9 bitcast_add_fusion
  96.1 0.7 copy.9
Async XLA Ops:
  0.6 1.7 %copy-start = (f32[2,10,1,128,256]{4,3,2,1,0:T(8,128)S(1)}, f32[2,10,1,128,256]{4,3,2,1,0:T(8,128)}, u32[]{:S(2)}) copy-start(f32[2,10,1,128,256]{4,3,2,1,0:T(8,128)} %param.6) | copy-start | bytes 7864324
  2.4 0.7 copy-start.1
  3.1 0.7 copy-start.2
  3.7 91.5 %copy-start.3 = (f32[2,256,256]{2,1,0:T(8,128)S(1)}, f32[2,256,256]{2,1,0:T(8,128)}, u32[]{:S(2)}) copy-start(f32[2,256,256]{2,1,0:T(8,128)} %param.9) | copy-start | bytes 1572868
